TPU v7x, 256 devices: a whole 4x4x8 slice. The times are simulated.
256 devices in a mesh: leaf: 64 (over y, z, core), rhs: 4 (over x).
Axes of the slice: x: 4, y: 4, z: 8, core: 2. Of those that a mesh axis runs over, the one named last changes fastest.
Arguments:
- leaf_right: float32 [2048, 256, 128], P('leaf', 'rhs'), may hold values from -6 to 6
- upper_right: float32 [128, 256, 128], P('leaf', 'rhs'), may hold values from -6 to 6
- leaf_inverse: bfloat16 [2048, 128, 128], P(('leaf', 'rhs')), as said below
- upper_inverse: bfloat16 [128, 128, 128], P('leaf'), as said below
- update_blocks: bfloat16 [16384, 128, 128], P('leaf'), may hold values from -0.046875 to 0.046875
- block_target: int32 [16384, 1], P('leaf'), may hold values from 0 to 127; in each aligned block of 256 rows (0 to 255, 256 to 511, ...) at most 4 rows name the same one
- upper_place: int32 [128], replicated, may hold values from 0 to 127, each once
Outputs:
- leaf_solution: float32 [2048, 256, 128], P('leaf', 'rhs')
- upper_solution: float32 [128, 256, 128], P('leaf', 'rhs')
Inputs may be any that keep to these rules, and one draw needn't show every extreme that they name: `leaf_inverse`: lower triangular blocks, diagonal entries between 0.6 and 1.4. `upper_inverse`: lower triangular blocks, diagonal entries between 0.6 and 1.4. `block_target`: among the 256 blocks of one device no upper supernode is named more than 4 times, a bound that some block reaches. `upper_place`: each row of the upper arrays holds exactly one upper supernode.
All inputs are finite; a program needn't handle non-finite values.
Results may differ from a plain program's by a relative error of at most 0.0049.
Values may be sent and summed in bfloat16 or wider, within the bound.
A program may use at most 64 MiB of HBM per device.

v0:
```python
import jax
import jax.numpy as jnp
from jax import lax
from jax.sharding import PartitionSpec as P


def on_device(
    leaf_right, upper_right, leaf_inverse, upper_inverse, update_blocks, block_target, upper_place
):
    inverse_mine = lax.all_gather(leaf_inverse, "rhs", axis=0, tiled=True)
    leaf_rounded = leaf_right.astype(jnp.bfloat16)
    leaf_forward = jnp.einsum(
        "ncw,nvw->ncv", leaf_rounded, inverse_mine, preferred_element_type=jnp.float32
    )
    leaf_half = leaf_forward.astype(jnp.bfloat16)
    leaf_count, columns, width = leaf_forward.shape
    block_count = update_blocks.shape[0]
    per_leaf = block_count // leaf_count
    grouped = update_blocks.reshape(leaf_count, per_leaf, width, width)
    updates = jnp.einsum("ncw,nbvw->nbcv", leaf_half, grouped, preferred_element_type=jnp.float32)
    updates = updates.reshape(block_count, columns, width)
    upper_total = upper_place.shape[0]
    table = jnp.arange(upper_total, dtype=jnp.int32)
    position = jnp.sum(jnp.where(block_target == table[None, :], upper_place[None, :], 0), axis=1)
    upper_rows = upper_right.shape[0]
    local_index = position
    inside = (local_index >= 0) & (local_index < upper_rows * lax.axis_size("leaf"))
    local_index = jnp.where(inside, local_index, upper_rows * lax.axis_size("leaf"))
    upper_sums = lax.psum_scatter(
        jax.ops.segment_sum(updates, local_index, num_segments=upper_rows * lax.axis_size("leaf")),
        "leaf",
        scatter_dimension=0,
        tiled=True,
    )
    upper_rounded = (upper_right - upper_sums).astype(jnp.bfloat16)
    upper_half = jnp.einsum(
        "pcw,pvw->pcv", upper_rounded, upper_inverse, preferred_element_type=jnp.float32
    ).astype(jnp.bfloat16)
    upper_solution = jnp.einsum(
        "pcw,pwv->pcv", upper_half, upper_inverse, preferred_element_type=jnp.float32
    )
    upper_sent = upper_solution.astype(jnp.bfloat16)
    solved_table = lax.all_gather(upper_sent, "leaf", axis=0, tiled=True)
    chosen = jnp.take(solved_table, position, axis=0)
    corrections = jnp.einsum(
        "kcv,kvw->kcw", chosen, update_blocks, preferred_element_type=jnp.float32
    )
    corrections = corrections.reshape(leaf_count, per_leaf, columns, width).sum(axis=1)
    leaf_back = (leaf_forward - corrections).astype(jnp.bfloat16)
    leaf_solution = jnp.einsum(
        "ncw,nwv->ncv", leaf_back, inverse_mine, preferred_element_type=jnp.float32
    )
    return (leaf_solution, upper_solution)


def solution(mesh):
    return jax.shard_map(
        on_device,
        mesh=mesh,
        in_specs=(
            P("leaf", "rhs", None),
            P("leaf", "rhs", None),
            P(("leaf", "rhs"), None, None),
            P("leaf", None, None),
            P("leaf", None, None),
            P("leaf", None),
            P(),
        ),
        out_specs=(P("leaf", "rhs", None), P("leaf", "rhs", None)),
        check_vma=False,
    )
```

profile of v0, /device:TPU:1, one launch (start us, length us, event | category | flops | bytes accessed | tf_op | source)
XLA Modules:
  0.0 338.4 jit_solution(17346281940933567968)
XLA Ops:
  7.2 0.0 copy-start
  7.2 0.0 all-gather.3.cloned.1.call-start
  7.2 0.7 all-gather.3.cloned.1.call-update
  7.9 0.0 reduce-scatter.2.cloned.1.call-start
  8.0 0.9 select_reduce_fusion
  8.8 30.4 %all-gather.3.cloned.1.call-done = bf16[32,128,128]{2,1,0:T(8,128)(2,1)} async-done(((bf16[8,128,128]{2,1,0:T(8,128)(2,1)}), bf16[32,128,128]{2,1,0:T(8,128)(2,1)}) %all-gather.3.cloned.1.call-update) | async-done | bytes 1048592 | tf_op jit(solution)/shard_map/all_gather | solution.py:10
  39.2 2.3 fusion.11
  41.6 9.6 %fusion.8 = f32[32,64,8,128]{3,1,2,0:T(8,128)} fusion(bf16[32,8,128,128]{3,2,1,0:T(8,128)(2,1)} %bitcast.22, f32[32,64,128]{2,1,0:T(8,128)S(1)} %fusion.11), kind=kOutput, calls=%fused_computation.11 | convolution fusion | flops 537133056 | bytes 17825792 | tf_op jit(solution)/shard_map/ncw,nbvw->nbcv/dot_general | solution.py:20
  51.2 2.5 broadcast_in_dim.33
  53.7 39.9 %scatter_fusion = f32[128,64,128]{2,1,0:T(8,128)} fusion(f32[128,64,128]{2,1,0:T(8,128)} %broadcast_in_dim.33, s32[256]{0:T(256)S(1)} %bitcast.23, f32[256,64,128]{2,1,0:T(8,128)} %bitcast.21), kind=kCustom, calls=%fused_computation.1 | custom fusion | flops 2097152 | bytes 25166848 | tf_op jit(solution)/shard_map/scatter-add | solution.py:30
  93.6 0.0 copy-start.2
  93.6 0.0 reduce-scatter.2.cloned.1.call-update
  93.6 0.0 all-gather.5.cloned.1.call-start
  93.7 140.1 %reduce-scatter.2.cloned.1.call-done = f32[2,64,128]{2,1,0:T(8,128)} async-done(((f32[128,64,128]{2,1,0:T(8,128)}), f32[2,64,128]{2,1,0:T(8,128)}) %reduce-scatter.2.cloned.1.call-update) | async-done | bytes 65552 | tf_op jit(solution)/shard_map/reduce_scatter | solution.py:29
  233.8 0.0 copy-done
  233.8 0.0 copy-done.2
  233.8 1.7 fusion.14
  235.5 0.0 all-gather.5.cloned.1.call-update
  235.6 83.0 %all-gather.5.cloned.1.call-done = bf16[128,64,128]{2,1,0:T(8,128)(2,1)} async-done(((bf16[2,64,128]{2,1,0:T(8,128)(2,1)}), bf16[128,64,128]{2,1,0:T(8,128)(2,1)}) %all-gather.5.cloned.1.call-update) | async-done | bytes 2097168 | tf_op jit(solution)/shard_map/all_gather | solution.py:43
  318.6 4.6 %gather_fusion = bf16[256,64,128]{2,1,0:T(8,128)(2,1)} fusion(bf16[128,64,128]{2,1,0:T(8,128)(2,1)} %all-gather.5.cloned.1.call-done, s32[1024]{0:T(1024)S(1)} %pad_clamp_fusion), kind=kCustom, calls=%fused_computation | custom fusion | bytes 8389632 | tf_op jit(solution)/shard_map/jit(_take)/gather | solution.py:44
  323.3 0.0 copy-start.1
  323.3 7.2 %bitcast_reduce_fusion = f32[32,64,128]{2,1,0:T(8,128)S(1)} fusion(bf16[256,128,128]{2,1,0:T(8,128)(2,1)} %param.11, bf16[256,64,128]{2,1,0:T(8,128)(2,1)} %gather_fusion, pred[256]{0:T(512)(128)(4,1)S(1)} %compare_and_fusion), kind=kOutput, calls=%fused_computation.2 | convolution fusion | flops 540803072 | bytes 13631744 | tf_op jit(solution)/shard_map/kcv,kvw->kcw/dot_general | solution.py:45
  330.4 0.0 copy-done.1
  330.4 1.4 fusion.7
  (3 shorter events, 0.0 us)
Async XLA Ops:
  7.2 226.6 %copy-start = (bf16[2,128,128]{2,1,0:T(8,128)(2,1)S(1)}, bf16[2,128,128]{2,1,0:T(8,128)(2,1)}, u32[]{:S(2)}) copy-start(bf16[2,128,128]{2,1,0:T(8,128)(2,1)} %param.10) | copy-start | bytes 196612
  7.2 32.1 %all-gather.3.cloned.1.call-start = ((), (), s32[]{:S(2)}) async-start(), calls=%async_computation.1 | async-start | bytes 1310720 | tf_op jit(solution)/shard_map/all_gather | solution.py:10
  7.9 225.9 %reduce-scatter.2.cloned.1.call-start = ((), (), s32[]{:S(2)}) async-start(), calls=%async_computation.2 | async-start | bytes 4259840 | tf_op jit(solution)/shard_map/reduce_scatter | solution.py:29
  93.6 140.2 %copy-start.2 = (f32[2,64,128]{2,1,0:T(8,128)S(1)}, f32[2,64,128]{2,1,0:T(8,128)}, u32[]{:S(2)}) copy-start(f32[2,64,128]{2,1,0:T(8,128)} %param.8) | copy-start | bytes 196612
  93.6 225.0 %all-gather.5.cloned.1.call-start = ((), (), s32[]{:S(2)}) async-start(), calls=%async_computation.3 | async-start | bytes 2129920 | tf_op jit(solution)/shard_map/all_gather | solution.py:43
  323.3 7.2 %copy-start.1 = (bf16[32,128,128]{2,1,0:T(8,128)(2,1)S(1)}, bf16[32,128,128]{2,1,0:T(8,128)(2,1)}, u32[]{:S(2)}) copy-start(bf16[32,128,128]{2,1,0:T(8,128)(2,1)} %all-gather.3.cloned.1.call-done) | copy-start | bytes 3145732
Sparse Core Ops, SparseCore 0:
  9.8 29.3 all-gather.2
  93.8 139.9 reduce-scatter.1
  237.5 81.0 all-gather.4
where the time goes:
time: 339 us; the launch traced here: 338 us
  waiting for transfers between devices  254 us (75%)
  other arithmetic  40.8 us (12%)
  matrix products  22.3 us (7%)
  between operations  13.8 us (4%)
  local copies, waits for them, and re-layouts  7.11 us (2%)
    reduce_scatter x1, waiting for transfers between devices, on_device(): lax.psum_scatter(jax.ops.segment_sum(updates, local_index, num_segments=u...  140 us
    all_gather x1, waiting for transfers between devices, on_device(): solved_table = lax.all_gather(upper_sent, 'leaf', axis=0, tiled=True)  83 us
    scatter-add x1, other arithmetic, on_device(): jax.ops.segment_sum(updates, local_index, num_segments=upper_rows * lax.a...  39.9 us
    all_gather x1, waiting for transfers between devices, on_device(): inverse_mine = lax.all_gather(leaf_inverse, 'rhs', axis=0, tiled=True)  30.4 us
    dot_general x1, matrix products, on_device(): jnp.einsum('ncw,nbvw->nbcv', leaf_half, grouped, preferred_element_type=j...  9.63 us
    dot_general x1, matrix products, on_device(): jnp.einsum('kcv,kvw->kcw', chosen, update_blocks, preferred_element_type=...  7.16 us
  transfers between devices with their start and end apart: 3, of which 3 were waited for; matrix products, arithmetic and copies ran while one was open for 0% of the time, Pallas kernels for 0%

commit v1 on v0

--- a/solution.py
+++ b/solution.py
@@ -1,13 +1,32 @@
+import functools
 import jax
 import jax.numpy as jnp
 from jax import lax
 from jax.sharding import PartitionSpec as P
 
 
+def read_meshes(patch, dim_k):
+    axis_len = jax.lax.psum(1, axis_name="rhs")
+    pieces_in = list(map(lambda dev: (dev, (dev + 1) % axis_len), range(axis_len)))
+
+    def end_rails_by_axis(even):
+        if len(even) == axis_len:
+            return even
+        return end_rails_by_axis(
+            [jax.lax.ppermute(even[0], axis_name="rhs", perm=pieces_in), *even]
+        )
+
+    upper = jnp.concatenate(end_rails_by_axis([patch]), axis=dim_k)
+    return jnp.roll(upper, (jax.lax.axis_index("rhs") + 1) * patch.shape[dim_k], axis=dim_k)
+
+
+_end_slices = functools.partial(read_meshes, dim_k=0)
+
+
 def on_device(
     leaf_right, upper_right, leaf_inverse, upper_inverse, update_blocks, block_target, upper_place
 ):
-    inverse_mine = lax.all_gather(leaf_inverse, "rhs", axis=0, tiled=True)
+    inverse_mine = _end_slices(leaf_inverse)
     leaf_rounded = leaf_right.astype(jnp.bfloat16)
     leaf_forward = jnp.einsum(
         "ncw,nvw->ncv", leaf_rounded, inverse_mine, preferred_element_type=jnp.float32

time: 339 us -> 332 us (0.979)
  waiting for transfers between devices: 254 us -> 243 us
  starting transfers between devices: 0.12 us -> 4.71 us
    all_gather x1 -> x0, waiting for transfers between devices: 30.4 us -> none  [on_device(): inverse_mine = lax.all_gather(leaf_inverse, 'rhs', axis=0, tiled=True)]
    ppermute x0 -> x3, waiting for transfers between devices: none -> 15.4 us  [end_rails_by_axis(): jax.lax.ppermute(even[0], axis_name='rhs', perm=pieces_in)]
    reduce_scatter x1, waiting for transfers between devices: 140 us -> 145 us  [on_device(): lax.psum_scatter(jax.ops.segment_sum(updates, local_index, num_segments=u...]
    ppermute x0 -> x3, starting transfers between devices: none -> 4.63 us  [end_rails_by_axis(): jax.lax.ppermute(even[0], axis_name='rhs', perm=pieces_in)]
  transfers between devices with their start and end apart: 3 -> 5, of which waited for: 3 -> 5; matrix products, arithmetic and copies ran while one was open for 0% -> 0% of each run, Pallas kernels for 0% -> 0%
where the time goes in v1:
time: 332 us
  waiting for transfers between devices  243 us (73%)
  other arithmetic  40.3 us (12%)
  matrix products  20.7 us (6%)
  between operations  14.2 us (4%)
  local copies, waits for them, and re-layouts  8.35 us (3%)
  starting transfers between devices  4.71 us (1%)
    reduce_scatter x1, waiting for transfers between devices, on_device(): lax.psum_scatter(jax.ops.segment_sum(updates, local_index, num_segments=u...  145 us
    all_gather x1, waiting for transfers between devices, on_device(): solved_table = lax.all_gather(upper_sent, 'leaf', axis=0, tiled=True)  83.1 us
    scatter-add x1, other arithmetic, on_device(): jax.ops.segment_sum(updates, local_index, num_segments=upper_rows * lax.a...  39.4 us
    ppermute x3, waiting for transfers between devices, end_rails_by_axis(): jax.lax.ppermute(even[0], axis_name='rhs', perm=pieces_in)  15.4 us
    dot_general x1, matrix products, on_device(): jnp.einsum('ncw,nbvw->nbcv', leaf_half, grouped, preferred_element_type=j...  9.63 us
    dot_general x1, matrix products, on_device(): jnp.einsum('kcv,kvw->kcw', chosen, update_blocks, preferred_element_type=...  7.1 us
  transfers between devices with their start and end apart: 5, of which 5 were waited for; matrix products, arithmetic and copies ran while one was open for 0% of the time, Pallas kernels for 0%

profile of v1, /device:TPU:1, one launch (start us, length us, event | category | flops | bytes accessed | tf_op | source)
XLA Modules:
  0.0 331.6 jit_solution(13001336889936337749)
XLA Ops:
  7.2 0.0 copy-start
  7.2 0.0 copy-start.2
  7.2 0.0 reduce-scatter.2.cloned.1.call-start
  7.2 2.1 collective-permute-start
  9.4 5.2 %collective-permute-done = bf16[8,128,128]{2,1,0:T(8,128)(2,1)S(1)} collective-permute-done((bf16[8,128,128]{2,1,0:T(8,128)(2,1)}, bf16[8,128,128]{2,1,0:T(8,128)(2,1)S(1)}, u32[]{:S(2)}, u32[]{:S(2)}) %collective-permute-start) | collective-permute-done | bytes 262176 | tf_op jit(solution)/shard_map/ppermute | solution.py:16
  14.6 1.9 collective-permute-start.1
  16.5 5.3 %collective-permute-done.1 = bf16[8,128,128]{2,1,0:T(8,128)(2,1)S(1)} collective-permute-done((bf16[8,128,128]{2,1,0:T(8,128)(2,1)S(1)}, bf16[8,128,128]{2,1,0:T(8,128)(2,1)S(1)}, u32[]{:S(2)}, u32[]{:S(2)}) %collective-permute-start.1) | collective-permute-done | bytes 262176 | tf_op jit(solution)/shard_map/ppermute | solution.py:16
  21.8 0.7 collective-permute-start.2
  22.4 0.9 select_reduce_fusion
  23.3 0.0 copy-start.1
  23.3 4.9 %collective-permute-done.2 = bf16[8,128,128]{2,1,0:T(8,128)(2,1)S(1)} collective-permute-done((bf16[8,128,128]{2,1,0:T(8,128)(2,1)S(1)}, bf16[8,128,128]{2,1,0:T(8,128)(2,1)S(1)}, u32[]{:S(2)}, u32[]{:S(2)}) %collective-permute-start.2) | collective-permute-done | bytes 262176 | tf_op jit(solution)/shard_map/ppermute | solution.py:16
  28.3 1.0 constant_dynamic-update-slice_fusion.4
  29.4 0.0 copy-done.2
  29.5 0.0 copy-done.1
  29.5 0.8 convolution_bitcast_fusion
  30.3 9.6 %fusion.10 = f32[32,64,8,128]{3,1,2,0:T(8,128)} fusion(bf16[32,8,128,128]{3,2,1,0:T(8,128)(2,1)} %bitcast.22, f32[32,64,128]{2,1,0:T(8,128)S(1)} %convolution_bitcast_fusion), kind=kOutput, calls=%fused_computation.14 | convolution fusion | flops 537133056 | bytes 17825792 | tf_op jit(solution)/shard_map/ncw,nbvw->nbcv/dot_general | solution.py:39
  40.0 2.5 broadcast_in_dim.33
  42.4 39.4 %scatter_fusion = f32[128,64,128]{2,1,0:T(8,128)} fusion(f32[128,64,128]{2,1,0:T(8,128)} %broadcast_in_dim.33, s32[256]{0:T(256)S(1)} %bitcast.23, f32[256,64,128]{2,1,0:T(8,128)} %bitcast.21), kind=kCustom, calls=%fused_computation.1 | custom fusion | flops 2097152 | bytes 25166848 | tf_op jit(solution)/shard_map/scatter-add | solution.py:49
  81.8 0.0 copy-start.3
  81.8 0.0 reduce-scatter.2.cloned.1.call-update
  81.8 0.0 all-gather.2.cloned.1.call-start
  81.9 144.8 %reduce-scatter.2.cloned.1.call-done = f32[2,64,128]{2,1,0:T(8,128)} async-done(((f32[128,64,128]{2,1,0:T(8,128)}), f32[2,64,128]{2,1,0:T(8,128)}) %reduce-scatter.2.cloned.1.call-update) | async-done | bytes 65552 | tf_op jit(solution)/shard_map/reduce_scatter | solution.py:48
  226.7 0.0 copy-done
  226.7 0.0 copy-done.3
  226.7 1.7 fusion.17
  228.5 0.0 all-gather.2.cloned.1.call-update
  228.5 83.1 %all-gather.2.cloned.1.call-done = bf16[128,64,128]{2,1,0:T(8,128)(2,1)} async-done(((bf16[2,64,128]{2,1,0:T(8,128)(2,1)}), bf16[128,64,128]{2,1,0:T(8,128)(2,1)}) %all-gather.2.cloned.1.call-update) | async-done | bytes 2097168 | tf_op jit(solution)/shard_map/all_gather | solution.py:62
  311.6 4.6 %gather_fusion = bf16[256,64,128]{2,1,0:T(8,128)(2,1)} fusion(bf16[128,64,128]{2,1,0:T(8,128)(2,1)} %all-gather.2.cloned.1.call-done, s32[1024]{0:T(1024)S(1)} %pad_clamp_fusion), kind=kCustom, calls=%fused_computation | custom fusion | bytes 8389632 | tf_op jit(solution)/shard_map/jit(_take)/gather | solution.py:63
  316.2 7.1 %bitcast_reduce_fusion = f32[32,64,128]{2,1,0:T(8,128)S(1)} fusion(bf16[256,128,128]{2,1,0:T(8,128)(2,1)} %param.11, bf16[256,64,128]{2,1,0:T(8,128)(2,1)} %gather_fusion, pred[256]{0:T(512)(128)(4,1)S(1)} %compare_and_fusion), kind=kOutput, calls=%fused_computation.2 | convolution fusion | flops 540803072 | bytes 13631744 | tf_op jit(solution)/shard_map/kcv,kvw->kcw/dot_general | solution.py:64
  323.3 1.4 fusion.7
  (10 shorter events, 0.3 us)
Async XLA Ops:
  7.2 219.6 %copy-start = (bf16[2,128,128]{2,1,0:T(8,128)(2,1)S(1)}, bf16[2,128,128]{2,1,0:T(8,128)(2,1)}, u32[]{:S(2)}) copy-start(bf16[2,128,128]{2,1,0:T(8,128)(2,1)} %param.10) | copy-start | bytes 196612
  7.2 22.3 %copy-start.2 = (bf16[8,128,128]{2,1,0:T(8,128)(2,1)S(1)}, bf16[8,128,128]{2,1,0:T(8,128)(2,1)}, u32[]{:S(2)}) copy-start(bf16[8,128,128]{2,1,0:T(8,128)(2,1)} %param.9) | copy-start | bytes 786436
  7.2 219.5 %reduce-scatter.2.cloned.1.call-start = ((), (), s32[]{:S(2)}) async-start(), calls=%async_computation.1 | async-start | bytes 4259840 | tf_op jit(solution)/shard_map/reduce_scatter | solution.py:48
  7.2 7.4 %collective-permute-start = (bf16[8,128,128]{2,1,0:T(8,128)(2,1)}, bf16[8,128,128]{2,1,0:T(8,128)(2,1)S(1)}, u32[]{:S(2)}, u32[]{:S(2)}) collective-permute-start(bf16[8,128,128]{2,1,0:T(8,128)(2,1)} %param.9), channel_id=1, source_target_pairs={{0,1},{1,2},{2,3},{3,0},{4,5},{5,6},{6,7},{7,4},{8,9},{9,10},{10,1... | collective-permute-start | bytes 786440 | tf_op jit(solution)/shard_map/ppermute | solution.py:16
  14.6 7.2 %collective-permute-start.1 = (bf16[8,128,128]{2,1,0:T(8,128)(2,1)S(1)}, bf16[8,128,128]{2,1,0:T(8,128)(2,1)S(1)}, u32[]{:S(2)}, u32[]{:S(2)}) collective-permute-start(bf16[8,128,128]{2,1,0:T(8,128)(2,1)S(1)} %collective-permute-done), channel_id=1, source_target_pairs={{0,1},{1,2},{2,3},{3,0},{4,5},{5,6},{6,7},{7,4},{8,9},{9,10},{10,1... | collective-permute-start | bytes 786440 | tf_op jit(solution)/shard_map/ppermute | solution.py:16
  21.8 6.4 %collective-permute-start.2 = (bf16[8,128,128]{2,1,0:T(8,128)(2,1)S(1)}, bf16[8,128,128]{2,1,0:T(8,128)(2,1)S(1)}, u32[]{:S(2)}, u32[]{:S(2)}) collective-permute-start(bf16[8,128,128]{2,1,0:T(8,128)(2,1)S(1)} %collective-permute-done.1), channel_id=1, source_target_pairs={{0,1},{1,2},{2,3},{3,0},{4,5},{5,6},{6,7},{7,4},{8,9},{9,10},{10,1... | collective-permute-start | bytes 786440 | tf_op jit(solution)/shard_map/ppermute | solution.py:16
  23.3 6.2 %copy-start.1 = (f32[32,64,128]{2,1,0:T(8,128)S(1)}, f32[32,64,128]{2,1,0:T(8,128)}, u32[]{:S(2)}) copy-start(f32[32,64,128]{2,1,0:T(8,128)} %param.7) | copy-start | bytes 3145732
  81.8 144.9 %copy-start.3 = (f32[2,64,128]{2,1,0:T(8,128)S(1)}, f32[2,64,128]{2,1,0:T(8,128)}, u32[]{:S(2)}) copy-start(f32[2,64,128]{2,1,0:T(8,128)} %param.8) | copy-start | bytes 196612
  81.8 229.7 %all-gather.2.cloned.1.call-start = ((), (), s32[]{:S(2)}) async-start(), calls=%async_computation.2 | async-start | bytes 2129920 | tf_op jit(solution)/shard_map/all_gather | solution.py:62
Sparse Core Ops, SparseCore 0:
  82.0 144.7 reduce-scatter.1
  230.5 81.0 all-gather.1
